TPU v7x, 32 devices: a whole 2x2x4 slice. The times are simulated.
32 devices in a mesh: pair: 8 (over z, x), cell: 4 (over y, core).
Axes of the slice: x: 2, y: 2, z: 4, core: 2. Of those that a mesh axis runs over, the one named last changes fastest.
Arguments:
- expression: bfloat16 [2048, 2048], P('cell', 'pair')
- plan: int32 [16], replicated, may hold values from 0 to 15, each once
- screen: int32 [4, 8], replicated, may hold values 0 or 1
Outputs:
- information: float32 [4, 1024, 128], P(None, ('pair', 'cell'))
Inputs may be any that keep to these rules, and one draw needn't show every extreme that they name: `plan`: a permutation of the 16 block numbers.
All inputs are finite; a program needn't handle non-finite values.
Results may differ from a plain program's by a relative error of at most 0.0021.
Values may be sent and summed in bfloat16 or wider, within the bound.
A program may use at most 128 MiB of HBM per device.

v0:
```python
import jax
import jax.numpy as jnp
from jax import lax
from jax.sharding import PartitionSpec as P

BINS = 10
BLOCK = 128
ROUNDS = 4


def from_behind(shard, axis, by):
    length = lax.axis_size(axis)
    pairs = [(i, i + by) for i in range(length) if 0 <= i + by < length]
    return lax.ppermute(shard, axis, pairs)


def cubic_basis(scaled):
    top = float(BINS - 3)
    knot_list = [0.0, 0.0, 0.0] + [float(v) for v in range(BINS - 2)] + [top, top, top]
    level = [
        ((scaled >= knot_list[i]) & (scaled < knot_list[i + 1])).astype(jnp.float32)
        for i in range(len(knot_list) - 1)
    ]
    for k in range(2, 5):
        nextlevel = []
        for i in range(len(level) - 1):
            term = jnp.zeros_like(scaled)
            first_gap = knot_list[i + k - 1] - knot_list[i]
            if first_gap > 0:
                term = (scaled - knot_list[i]) / first_gap * level[i]
            second_gap = knot_list[i + k] - knot_list[i + 1]
            if second_gap > 0:
                term = term + (knot_list[i + k] - scaled) / second_gap * level[i + 1]
            nextlevel.append(term)
        level = nextlevel
    return level


def spline_weights(values):
    scaled = (BINS - 3) * jax.nn.sigmoid(values.astype(jnp.float32))
    basis = jnp.stack(cubic_basis(scaled), -1)
    return basis.reshape(values.shape[0], values.shape[1] * BINS).astype(jnp.bfloat16)


def entropy_terms(v):
    return v * jnp.log(jnp.maximum(v, 1e-30))


def mutual_information(histogram, cell_total):
    joint = histogram / cell_total
    genes_left = joint.shape[0] // BINS
    joint = joint.reshape(genes_left, BINS, BLOCK, BINS)
    whole = entropy_terms(joint).sum(axis=(1, 3))
    left = joint.sum(3)
    right = joint.sum(1)
    return whole - entropy_terms(left).sum(1) - entropy_terms(right).sum(2)


def local(expression, plan, screen):
    pair_count = lax.axis_size("pair")
    cell_count = lax.axis_size("cell")
    pair_index = lax.axis_index("pair")
    cell_rows = expression.shape[0]
    cell_total = cell_rows * cell_count
    wanted_pair = plan.reshape(-1, 2)[pair_index]
    slot_blocks = jnp.where(jnp.arange(2 * BLOCK) < BLOCK, wanted_pair[0], wanted_pair[1])
    slot_offset = jnp.arange(2 * BLOCK) % BLOCK
    piece = lax.all_gather(expression, "pair", axis=1, tiled=True)
    column = jnp.arange(piece.shape[1])
    owner_block = column // BLOCK
    offset = column % BLOCK
    selector = (
        (owner_block[:, None] == slot_blocks[None, :]) & (offset[:, None] == slot_offset[None, :])
    ).astype(jnp.bfloat16)
    seated = jnp.dot(piece, selector, preferred_element_type=jnp.float32).astype(jnp.bfloat16)
    first_values = seated[:, :BLOCK]
    second_values = seated[:, BLOCK:]
    first_carried = spline_weights(first_values)
    second_carried = spline_weights(second_values)
    results = []
    for round_index in range(ROUNDS):
        if round_index > 0:
            leaving = jnp.where(pair_index == 0, second_carried, first_carried)
            arriving = from_behind(leaving, "pair", 1)
            returning = from_behind(second_carried, "pair", -1)
            new_first = jnp.where(pair_index == 0, first_carried, arriving)
            new_second = jnp.where(pair_index == pair_count - 1, first_carried, returning)
            first_carried = new_first
            second_carried = new_second
        histogram = lax.psum_scatter(
            lax.dot_general(
                first_carried,
                second_carried,
                (((0,), (0,)), ((), ())),
                preferred_element_type=jnp.float32,
            ),
            "cell",
            scatter_dimension=0,
            tiled=True,
        )
        values = mutual_information(histogram, cell_total)
        values = jnp.where(screen[round_index, pair_index] == 1, values, jnp.float32(0.0))
        results.append(values)
    return jnp.stack(results)


def solution(mesh):
    placed = (P("cell", "pair"), P(), P())
    return jax.shard_map(
        local,
        mesh=mesh,
        in_specs=placed,
        out_specs=P(None, ("pair", "cell"), None),
        check_vma=False,
    )
```

profile of v0, /device:TPU:0, one launch (start us, length us, event | category | flops | bytes accessed | tf_op | source)
XLA Modules:
  0.0 456.5 jit_solution(1655143068081047137)
XLA Ops:
  6.5 0.7 all-gather.2.cloned.1.call-update
  7.3 0.7 reshape.185
  8.0 0.6 fusion.54
  8.6 1.3 and_select_fusion.2
  9.9 53.3 %all-gather.2.cloned.1.call-done = bf16[512,2048]{1,0:T(8,128)(2,1)} async-done(((bf16[512,256]{1,0:T(8,128)(2,1)}), bf16[512,2048]{1,0:T(8,128)(2,1)}) %all-gather.2.cloned.1.call-update) | async-done | bytes 2097168 | tf_op jit(solution)/shard_map/all_gather | solution.py:68
  63.2 2.9 fusion.5
  66.3 0.2 fusion.37
  66.5 0.3 bitcast_dynamic-update-slice_fusion.5
  66.8 0.4 bitcast_dynamic-update-slice_fusion.4
  67.2 0.4 bitcast_dynamic-update-slice_fusion.3
  67.7 0.4 bitcast_dynamic-update-slice_fusion.2
  68.1 0.4 bitcast_dynamic-update-slice_fusion.1
  68.5 0.5 bitcast_dynamic-update-slice_fusion
  69.0 0.5 fusion.18
  69.4 0.5 fusion.20
  69.9 1.0 copy-done.2
  70.9 0.8 copy.37
  71.8 1.3 convert_element_type.60
  73.1 1.0 bitcast_dynamic-update-slice_fusion.10
  74.1 1.0 bitcast_dynamic-update-slice_fusion.9
  75.2 1.1 bitcast_dynamic-update-slice_fusion.8
  76.3 1.1 bitcast_dynamic-update-slice_fusion.7
  77.3 1.0 bitcast_dynamic-update-slice_fusion.6
  78.3 0.9 fusion.23
  79.2 0.8 fusion.25
  79.9 3.5 copy.36
  83.4 2.7 convert_element_type.57
  86.1 4.6 %fusion.55 = f32[1280,1280]{1,0:T(8,128)} fusion(bf16[512,1280]{0,1:T(8,128)(2,1)S(1)} %convert_element_type.57, bf16[512,1280]{0,1:T(8,128)(2,1)S(1)} %copy-done.1), kind=kOutput, calls=%fused_computation.160 | convolution fusion | flops 1677721600 | bytes 9175040 | tf_op jit(solution)/shard_map/dot_general | solution.py:91
  90.8 1.2 broadcast_select_fusion.6
  92.0 4.4 collective-permute-start
  96.4 1.5 collective-permute-start.1
  97.9 54.1 %collective-permute-done = bf16[512,1280]{0,1:T(8,128)(2,1)} collective-permute-done((bf16[512,1280]{0,1:T(8,128)(2,1)}, bf16[512,1280]{0,1:T(8,128)(2,1)}, u32[]{:S(2)}, u32[]{:S(2)}) %collective-permute-start) | collective-permute-done | bytes 1310752 | tf_op jit(solution)/shard_map/ppermute | solution.py:14
  152.0 2.6 broadcast_select_fusion.4
  154.6 1.1 copy-done.3
  155.7 4.6 %fusion.56 = f32[1280,1280]{1,0:T(8,128)} fusion(bf16[512,1280]{0,1:T(8,128)(2,1)S(1)} %get-tuple-element.21, bf16[512,1280]{0,1:T(8,128)(2,1)S(1)} %get-tuple-element.20), kind=kOutput, calls=%fused_computation.161 | convolution fusion | flops 1677721600 | bytes 9175040 | tf_op jit(solution)/shard_map/dot_general | solution.py:91
  160.3 4.9 %collective-permute-start.2 = (bf16[512,1280]{0,1:T(8,128)(2,1)}, bf16[512,1280]{0,1:T(8,128)(2,1)S(1)}, u32[]{:S(2)}, u32[]{:S(2)}) collective-permute-start(bf16[512,1280]{0,1:T(8,128)(2,1)} %get-tuple-element.19), channel_id=1, source_target_pairs={{0,4},{4,8},{8,12},{12,16},{16,20},{20,24},{24,28},{1,5},{5,9},{9,... | collective-permute-start | bytes 3932168 | tf_op jit(solution)/shard_map/ppermute | solution.py:14
  165.2 1.3 collective-permute-start.3
  166.5 54.4 %collective-permute-done.2 = bf16[512,1280]{0,1:T(8,128)(2,1)S(1)} collective-permute-done((bf16[512,1280]{0,1:T(8,128)(2,1)}, bf16[512,1280]{0,1:T(8,128)(2,1)S(1)}, u32[]{:S(2)}, u32[]{:S(2)}) %collective-permute-start.2) | collective-permute-done | bytes 1310752 | tf_op jit(solution)/shard_map/ppermute | solution.py:14
  221.0 1.4 broadcast_select_fusion.2
  222.3 1.1 copy-done
  223.5 4.6 %fusion.49 = f32[1280,1280]{1,0:T(8,128)} fusion(bf16[512,1280]{0,1:T(8,128)(2,1)S(1)} %get-tuple-element.18, bf16[512,1280]{0,1:T(8,128)(2,1)S(1)} %get-tuple-element.21, bf16[512,1280]{0,1:T(8,128)(2,1)S(1)} %collective-permute-done.2, pred[]{:T(512)S(6)} %eq.77), kind=kOutput, calls=%fused_computation.154 | convolution fusion | flops 1678376960 | bytes 10485761 | tf_op jit(solution)/shard_map/dot_general | solution.py:91
  228.2 4.4 collective-permute-start.4
  232.5 1.3 collective-permute-start.5
  233.8 53.5 %collective-permute-done.4 = bf16[512,1280]{0,1:T(8,128)(2,1)S(1)} collective-permute-done((bf16[512,1280]{0,1:T(8,128)(2,1)}, bf16[512,1280]{0,1:T(8,128)(2,1)S(1)}, u32[]{:S(2)}, u32[]{:S(2)}) %collective-permute-start.4) | collective-permute-done | bytes 1310752 | tf_op jit(solution)/shard_map/ppermute | solution.py:14
  287.3 4.8 %fusion = f32[1280,1280]{1,0:T(8,128)} fusion(bf16[512,1280]{0,1:T(8,128)(2,1)S(1)} %collective-permute-done.5, bf16[512,1280]{0,1:T(8,128)(2,1)S(1)} %collective-permute-done.4, pred[]{:T(512)S(6)} %eq.78, pred[]{:T(512)S(6)} %eq.77, bf16[512,1280]{0,1:T(8,128)(2,1)S(1)} %get-tuple-element.21, bf16[512,1280]{0,1:T(8,128)(2,1)S(1)} %collective-permute-done.2), kind=kOutput, calls=%fused_computation.5 | convolution fusion | flops 1680343040 | bytes 11796482 | tf_op jit(solution)/shard_map/dot_general | solution.py:91
  292.2 0.7 copy-done.4
  292.9 0.6 constant_dynamic-slice_fusion.3
  296.0 1.5 broadcast_multiply_fusion.3
  297.5 23.5 %reshape.186 = f32[32,10,128,10]{3,2,1,0:T(8,128)} reshape(f32[320,1280]{1,0:T(8,128)S(1)} %broadcast_multiply_fusion.3) | data formatting | bytes 3276800 | tf_op jit(solution)/shard_map/reshape | solution.py:52
  321.0 12.6 %fusion.50 = (f32[32,10,128]{2,1,0:T(8,128)S(1)}, f32[32,128]{1,0:T(8,128)S(1)}, f32[32,128,10]{2,1,0:T(8,128)S(1)}) fusion(f32[32,10,128,10]{3,2,1,0:T(8,128)} %reshape.186), kind=kLoop, calls=%fused_computation.155 | loop fusion | flops 1961984 | bytes 1982464 | tf_op jit(solution)/shard_map/reduce_sum | solution.py:54
  333.6 0.6 copy.41
  334.4 1.5 broadcast_multiply_fusion.2
  335.9 23.5 %reshape.187 = f32[32,10,128,10]{3,2,1,0:T(8,128)} reshape(f32[320,1280]{1,0:T(8,128)S(1)} %broadcast_multiply_fusion.2) | data formatting | bytes 3276800 | tf_op jit(solution)/shard_map/reshape | solution.py:52
  359.4 12.4 %fusion.51 = (f32[32,10,128]{2,1,0:T(8,128)S(1)}, f32[32,128]{1,0:T(8,128)S(1)}, f32[32,128,10]{2,1,0:T(8,128)S(1)}) fusion(f32[32,10,128,10]{3,2,1,0:T(8,128)} %reshape.187), kind=kLoop, calls=%fused_computation.156 | loop fusion | flops 1961984 | bytes 1982464 | tf_op jit(solution)/shard_map/reduce_sum | solution.py:54
  371.8 0.6 copy.45
  372.6 1.5 broadcast_multiply_fusion.1
  374.2 23.5 %reshape.188 = f32[32,10,128,10]{3,2,1,0:T(8,128)} reshape(f32[320,1280]{1,0:T(8,128)S(1)} %broadcast_multiply_fusion.1) | data formatting | bytes 3276800 | tf_op jit(solution)/shard_map/reshape | solution.py:52
  397.7 12.4 %fusion.52 = (f32[32,10,128]{2,1,0:T(8,128)S(1)}, f32[32,128]{1,0:T(8,128)S(1)}, f32[32,128,10]{2,1,0:T(8,128)S(1)}) fusion(f32[32,10,128,10]{3,2,1,0:T(8,128)} %reshape.188), kind=kLoop, calls=%fused_computation.157 | loop fusion | flops 1961984 | bytes 1982464 | tf_op jit(solution)/shard_map/reduce_sum | solution.py:54
  410.1 0.6 copy.49
  410.9 1.5 broadcast_multiply_fusion
  412.4 23.7 %reshape.189 = f32[32,10,128,10]{3,2,1,0:T(8,128)} reshape(f32[320,1280]{1,0:T(8,128)S(1)} %broadcast_multiply_fusion) | data formatting | bytes 3276800 | tf_op jit(solution)/shard_map/reshape | solution.py:52
  436.1 12.4 %fusion.53 = (f32[32,10,128]{2,1,0:T(8,128)S(1)}, f32[32,128]{1,0:T(8,128)S(1)}, f32[32,128,10]{2,1,0:T(8,128)S(1)}) fusion(f32[32,10,128,10]{3,2,1,0:T(8,128)} %reshape.189), kind=kLoop, calls=%fused_computation.158 | loop fusion | flops 1961984 | bytes 1982464 | tf_op jit(solution)/shard_map/reduce_sum | solution.py:54
  448.6 0.6 copy.53
  449.3 0.6 pad_maximum_fusion
  (37 shorter events, 1.0 us)
Async XLA Ops:
  6.5 56.7 %all-gather.2.cloned.1.call-start = ((), (), s32[]{:S(2)}) async-start(), calls=%async_computation.4 | async-start | bytes 2359296 | tf_op jit(solution)/shard_map/all_gather | solution.py:68
  7.3 288.7 %reduce-scatter.5.cloned.1.call-start = ((), (), s32[]{:S(2)}) async-start(), calls=%async_computation.5 | async-start | bytes 8192000 | tf_op jit(solution)/shard_map/reduce_scatter | solution.py:90
  69.9 1.1 copy-start.2
  83.4 2.7 copy-start.1
  90.8 243.6 %reduce-scatter.7.cloned.1.call-start = ((), (), s32[]{:S(2)}) async-start(), calls=%async_computation.6 | async-start | bytes 8192000 | tf_op jit(solution)/shard_map/reduce_scatter | solution.py:90
  92.0 60.0 %collective-permute-start = (bf16[512,1280]{0,1:T(8,128)(2,1)}, bf16[512,1280]{0,1:T(8,128)(2,1)}, u32[]{:S(2)}, u32[]{:S(2)}) collective-permute-start(bf16[512,1280]{0,1:T(8,128)(2,1)} %broadcast_select_fusion.6), channel_id=1, source_target_pairs={{0,4},{4,8},{8,12},{12,16},{16,20},{20,24},{24,28},{1,5},{5,9},{9,... | collective-permute-start | bytes 3932168 | tf_op jit(solution)/shard_map/ppermute | solution.py:14
  96.4 55.6 %collective-permute-start.1 = (bf16[512,1280]{0,1:T(8,128)(2,1)S(1)}, bf16[512,1280]{0,1:T(8,128)(2,1)}, u32[]{:S(2)}, u32[]{:S(2)}) collective-permute-start(bf16[512,1280]{0,1:T(8,128)(2,1)S(1)} %copy-done.1), channel_id=1, source_target_pairs={{4,0},{8,4},{12,8},{16,12},{20,16},{24,20},{28,24},{5,1},{9,5},{13... | collective-permute-start | bytes 3932168 | tf_op jit(solution)/shard_map/ppermute | solution.py:14
  154.6 1.1 copy-start.3
  160.3 212.3 %reduce-scatter.9.cloned.1.call-start = ((), (), s32[]{:S(2)}) async-start(), calls=%async_computation.7 | async-start | bytes 8192000 | tf_op jit(solution)/shard_map/reduce_scatter | solution.py:90
  160.3 60.6 %collective-permute-start.2 = (bf16[512,1280]{0,1:T(8,128)(2,1)}, bf16[512,1280]{0,1:T(8,128)(2,1)S(1)}, u32[]{:S(2)}, u32[]{:S(2)}) collective-permute-start(bf16[512,1280]{0,1:T(8,128)(2,1)} %get-tuple-element.19), channel_id=1, source_target_pairs={{0,4},{4,8},{8,12},{12,16},{16,20},{20,24},{24,28},{1,5},{5,9},{9,... | collective-permute-start | bytes 3932168 | tf_op jit(solution)/shard_map/ppermute | solution.py:14
  165.2 55.8 %collective-permute-start.3 = (bf16[512,1280]{0,1:T(8,128)(2,1)}, bf16[512,1280]{0,1:T(8,128)(2,1)S(1)}, u32[]{:S(2)}, u32[]{:S(2)}) collective-permute-start(bf16[512,1280]{0,1:T(8,128)(2,1)} %copy-done.3), channel_id=1, source_target_pairs={{4,0},{8,4},{12,8},{16,12},{20,16},{24,20},{28,24},{5,1},{9,5},{13... | collective-permute-start | bytes 3932168 | tf_op jit(solution)/shard_map/ppermute | solution.py:14
  222.3 1.1 copy-start
  228.1 182.8 %reduce-scatter.11.cloned.1.call-start = ((), (), s32[]{:S(2)}) async-start(), calls=%async_computation.8 | async-start | bytes 8192000 | tf_op jit(solution)/shard_map/reduce_scatter | solution.py:90
  228.2 59.2 %collective-permute-start.4 = (bf16[512,1280]{0,1:T(8,128)(2,1)}, bf16[512,1280]{0,1:T(8,128)(2,1)S(1)}, u32[]{:S(2)}, u32[]{:S(2)}) collective-permute-start(bf16[512,1280]{0,1:T(8,128)(2,1)} %get-tuple-element.17), channel_id=1, source_target_pairs={{0,4},{4,8},{8,12},{12,16},{16,20},{20,24},{24,28},{1,5},{5,9},{9,... | collective-permute-start | bytes 3932168 | tf_op jit(solution)/shard_map/ppermute | solution.py:14
  232.5 54.8 %collective-permute-start.5 = (bf16[512,1280]{0,1:T(8,128)(2,1)}, bf16[512,1280]{0,1:T(8,128)(2,1)S(1)}, u32[]{:S(2)}, u32[]{:S(2)}) collective-permute-start(bf16[512,1280]{0,1:T(8,128)(2,1)} %copy-done), channel_id=1, source_target_pairs={{4,0},{8,4},{12,8},{16,12},{20,16},{24,20},{28,24},{5,1},{9,5},{13... | collective-permute-start | bytes 3932168 | tf_op jit(solution)/shard_map/ppermute | solution.py:14
  292.2 0.7 copy-start.4
Sparse Core Ops, SparseCore 0:
  9.4 53.7 all-gather.1
  90.9 58.2 reduce-scatter.4
  160.4 60.5 reduce-scatter.6
  228.2 61.6 reduce-scatter.8
  292.5 64.1 reduce-scatter.10
where the time goes:
time: 461 us; the launch traced here: 457 us
  waiting for transfers between devices  216 us (47%)
  local copies, waits for them, and re-layouts  111 us (24%)
  other arithmetic  74.1 us (16%)
  matrix products  21.6 us (5%)
  starting transfers between devices  17.8 us (4%)
  between operations  15.9 us (3%)
    ppermute x6, waiting for transfers between devices, from_behind(): return lax.ppermute(shard, axis, pairs)  162 us
    reshape x4, local copies, waits for them, and re-layouts, mutual_information(): joint = joint.reshape(genes_left, BINS, BLOCK, BINS)  94.1 us
    all_gather x1, waiting for transfers between devices, local(): piece = lax.all_gather(expression, 'pair', axis=1, tiled=True)  53.3 us
    reduce_sum x4, other arithmetic, mutual_information(): left = joint.sum(3)  49.8 us
    dot_general x4, matrix products, local(): lax.dot_general(first_carried, second_carried, (((0,), (0,)), ((), ())),...  18.7 us
    ppermute x6, starting transfers between devices, from_behind(): return lax.ppermute(shard, axis, pairs)  17.7 us
    unnamed x15, other arithmetic  9.32 us
  transfers between devices with their start and end apart: 11, of which 4 were waited for; matrix products, arithmetic and copies ran while one was open for 30% of the time, Pallas kernels for 0%

commit v1 on v0

v1 whole, which is shorter than its diff:
```python
import functools

import jax
import jax.numpy as jnp
import numpy as np
from jax import lax
from jax.experimental import pallas as pl
from jax.experimental.pallas import tpu as pltpu
from jax.sharding import PartitionSpec as P

BINS = 10
BLOCK = 128
ROUNDS = 4


def seat_table(tables):
    firsts = [2 * p for p in range(tables)]
    seconds = [2 * p + 1 for p in range(tables)]
    out = np.zeros((tables, ROUNDS, 2), np.int32)
    for r in range(ROUNDS):
        if r > 0:
            firsts, seconds = firsts[:1] + seconds[:1] + firsts[1:-1], seconds[1:] + firsts[-1:]
        out[:, r, 0] = firsts
        out[:, r, 1] = seconds
    return out


def basis(x, scale):
    s = 7.0 * jax.nn.sigmoid(x.astype(jnp.float32))
    k = jnp.floor(s)
    t = s - k
    n = 1.0 - t
    zero = jnp.zeros_like(s)
    m = [k == float(v) for v in range(7)]

    def side(t):
        t2 = t * t
        cube = t2 * t * scale
        edge1 = t * ((3.0 * scale) + t * ((-4.5 * scale) + (1.75 * scale) * t))
        edge2 = t2 * ((1.5 * scale) - (11.0 / 12.0 * scale) * t)
        return t2, cube, edge1, edge2

    t2, t3, e1, e2 = side(t)
    n2, n3, g1, g2 = side(n)
    t6 = t3 * (1.0 / 6.0)
    n6 = n3 * (1.0 / 6.0)
    fall = (2.0 / 3.0 * scale) - t2 * scale + 0.5 * t3
    rise = (2.0 / 3.0 * scale) - n2 * scale + 0.5 * n3
    h = 1.0 + n
    u = 1.0 + t
    e2b = h * h * h * (scale / 6.0) - 0.75 * n3
    g2b = u * u * u * (scale / 6.0) - 0.75 * t3
    t4 = 0.25 * t3
    n4 = 0.25 * n3

    def pick(*pairs):
        value = zero
        for mask, piece in pairs:
            value = jnp.where(mask, piece, value)
        return value

    return [
        pick((m[0], n3)),
        pick((m[0], e1), (m[1], n4)),
        pick((m[0], e2), (m[1], e2b), (m[2], n6)),
        pick((m[0], t6), (m[1], rise), (m[2], fall), (m[3], n6)),
        pick((m[1], t6), (m[2], rise), (m[3], fall), (m[4], n6)),
        pick((m[2], t6), (m[3], rise), (m[4], fall), (m[5], n6)),
        pick((m[3], t6), (m[4], rise), (m[5], fall), (m[6], n6)),
        pick((m[4], t6), (m[5], g2b), (m[6], g2)),
        pick((m[5], t4), (m[6], g1)),
        pick((m[6], t3)),
    ]


def entropy_terms(v):
    return v * jnp.log(jnp.maximum(v, 1e-30))


def kernel(first_ref, second_ref, out_ref, wf, ws, part, left):
    cells = second_ref.shape[0]

    @pl.loop(0, cells // 128)
    def _(c):
        at = pl.ds(pl.multiple_of(c * 128, 128), 128)
        for g in range(0, 128, 32):
            vals = basis(first_ref[g:g + 32, at], 1.0)
            for i in range(BINS):
                wf[i * BLOCK + g:i * BLOCK + g + 32, at] = vals[i].astype(jnp.bfloat16)

    @pl.loop(0, cells // 32)
    def _(c):
        at = pl.ds(pl.multiple_of(c * 32, 32), 32)
        vals = basis(second_ref[at, :], 1.0 / cells)
        for i in range(BINS):
            ws[at, i * BLOCK:(i + 1) * BLOCK] = vals[i].astype(jnp.bfloat16)

    out_ref[...] = jnp.zeros_like(out_ref)
    left[...] = jnp.zeros_like(left)
    for j in range(BINS // 2):
        part[...] = jnp.dot(
            wf[...], ws[:, j * 2 * BLOCK:(j + 1) * 2 * BLOCK], preferred_element_type=jnp.float32
        )

        @pl.loop(0, BLOCK // 16)
        def _(g):
            base = pl.multiple_of(g * 16, 16)
            total = out_ref[pl.ds(base, 16), :]
            right0 = jnp.zeros((16, BLOCK), jnp.float32)
            right1 = right0
            for i in range(BINS):
                rows = pl.ds(i * BLOCK + base, 16)
                v0 = part[rows, :BLOCK]
                v1 = part[rows, BLOCK:]
                total += entropy_terms(v0) + entropy_terms(v1)
                right0 += v0
                right1 += v1
                left[rows, :] += v0 + v1
            total -= entropy_terms(right0) + entropy_terms(right1)
            out_ref[pl.ds(base, 16), :] = total

    @pl.loop(0, BLOCK // 16)
    def _(g):
        base = pl.multiple_of(g * 16, 16)
        total = out_ref[pl.ds(base, 16), :]
        for i in range(BINS):
            total -= entropy_terms(left[pl.ds(i * BLOCK + base, 16), :])
        out_ref[pl.ds(base, 16), :] = total


def pair_information(first, second):
    cells = second.shape[0]
    return pl.pallas_call(
        kernel,
        out_shape=jax.ShapeDtypeStruct((BLOCK, BLOCK), jnp.float32),
        in_specs=[pl.BlockSpec(memory_space=pltpu.VMEM)] * 2,
        out_specs=pl.BlockSpec(memory_space=pltpu.VMEM),
        scratch_shapes=[
            pltpu.VMEM((BINS * BLOCK, cells), jnp.bfloat16),
            pltpu.VMEM((cells, BINS * BLOCK), jnp.bfloat16),
            pltpu.VMEM((BINS * BLOCK, 2 * BLOCK), jnp.float32),
            pltpu.VMEM((BINS * BLOCK, BLOCK), jnp.float32),
        ],
        compiler_params=pltpu.CompilerParams(vmem_limit_bytes=48 * 1024 * 1024),
    )(first, second)


def local(expression, plan, screen):
    tables = lax.axis_size("pair")
    groups = lax.axis_size("cell")
    split = groups // ROUNDS
    table = lax.axis_index("pair")
    group = lax.axis_index("cell")
    rows = expression.shape[0]
    cells = rows * groups
    seats = jnp.asarray(seat_table(tables))[table]
    wanted = plan[seats]
    blocks = expression.reshape(rows, 2, BLOCK).transpose(1, 0, 2)
    blocks = lax.all_gather(blocks, "pair", axis=0, tiled=True)
    order = [r // split for r in range(groups)]
    parts = []
    for c in range(groups):
        for s in range(2):
            parts.append(lax.dynamic_index_in_dim(blocks, wanted[order[c], s], 0, keepdims=False))
    send = jnp.stack(parts).reshape(groups, 2, rows, BLOCK)
    got = lax.all_to_all(send, "cell", 0, 0, tiled=True)
    first = got[:, 0].reshape(cells, BLOCK).T
    second = got[:, 1].reshape(cells, BLOCK)
    mine = pair_information(first, second)
    mine = jnp.where(screen[group // split, table] == 1, mine, jnp.float32(0.0))
    share = BLOCK // groups
    if split == 1:
        return lax.all_to_all(mine.reshape(groups, share, BLOCK), "cell", 0, 0, tiled=True)
    every = lax.all_gather(mine, "cell", axis=0)[::split]
    return lax.dynamic_slice_in_dim(every, group * share, share, 1)


def solution(mesh):
    return jax.shard_map(
        local,
        mesh=mesh,
        in_specs=(P("cell", "pair"), P(), P()),
        out_specs=P(None, ("pair", "cell"), None),
        check_vma=False,
    )
```

time: 461 us -> 129 us (0.28)
  waiting for transfers between devices: 216 us -> 48.2 us
  local copies, waits for them, and re-layouts: 111 us -> 18.2 us
  other arithmetic: 74.1 us -> 0.71 us
  Pallas kernels: 0 us -> 22.5 us
  matrix products: 21.6 us -> 0 us
  starting transfers between devices: 17.8 us -> 3.52 us
  between operations: 15.9 us -> 29.2 us
  blocking collectives: 0 us -> 6.49 us
    ppermute x6 -> x0, waiting for transfers between devices: 162 us -> none  [from_behind(): return lax.ppermute(shard, axis, pairs)]
    reshape x5 -> x0, local copies, waits for them, and re-layouts: 94.9 us -> none  [the longest x4 94.1 us: mutual_information(): joint = joint.reshape(genes_left, BINS, BLOCK, BINS)]
    reduce_sum x12 -> x0, other arithmetic: 50.3 us -> none  [the longest x4 49.8 us: mutual_information(): left = joint.sum(3)]
    pallas_call x0 -> x1, Pallas kernels: none -> 22.5 us  [pair_information(): pl.pallas_call(kernel, out_shape=jax.ShapeDtypeStruct((BLOCK, BLOCK), jnp...]
    dot_general x5 -> x0, matrix products: 21.6 us -> none  [the longest x4 18.7 us: local(): lax.dot_general(first_carried, second_carried, (((0,), (0,)), ((), ())),...]
    ppermute x6 -> x0, starting transfers between devices: 17.7 us -> none  [from_behind(): return lax.ppermute(shard, axis, pairs)]
    all_gather x1, waiting for transfers between devices: 53.3 us -> 35.6 us  [local(): blocks = lax.all_gather(blocks, 'pair', axis=0, tiled=True)]
    all_to_all x0 -> x1, waiting for transfers between devices: none -> 12.5 us  [local(): got = lax.all_to_all(send, 'cell', 0, 0, tiled=True)]
  transfers between devices with their start and end apart: 11 -> 2, of which waited for: 4 -> 2; matrix products, arithmetic and copies ran while one was open for 30% -> 3% of each run, Pallas kernels for 0% -> 0%
where the time goes in v1:
time: 129 us
  waiting for transfers between devices  48.2 us (37%)
  between operations  29.2 us (23%)
  Pallas kernels  22.5 us (17%)
  local copies, waits for them, and re-layouts  18.2 us (14%)
  blocking collectives  6.49 us (5%)
  starting transfers between devices  3.52 us (3%)
    all_gather x1, waiting for transfers between devices, local(): blocks = lax.all_gather(blocks, 'pair', axis=0, tiled=True)  35.6 us
    pallas_call x1, Pallas kernels, pair_information(): pl.pallas_call(kernel, out_shape=jax.ShapeDtypeStruct((BLOCK, BLOCK), jnp...  22.5 us
    unnamed x11, local copies, waits for them, and re-layouts  12.6 us
    all_to_all x1, waiting for transfers between devices, local(): got = lax.all_to_all(send, 'cell', 0, 0, tiled=True)  12.5 us
    all_to_all x1, blocking collectives, local(): lax.all_to_all(mine.reshape(groups, share, BLOCK), 'cell', 0, 0, tiled=True)  6.49 us
    all_to_all x1, starting transfers between devices, local(): got = lax.all_to_all(send, 'cell', 0, 0, tiled=True)  3.51 us
  transfers between devices with their start and end apart: 2, of which 2 were waited for; matrix products, arithmetic and copies ran while one was open for 3% of the time, Pallas kernels for 0%

profile of v1, /device:TPU:0, one launch (start us, length us, event | category | flops | bytes accessed | tf_op | source)
XLA Modules:
  0.0 128.8 jit_solution(4336848184225076429)
XLA Ops:
  6.5 0.0 copy-start
  6.5 0.0 all-gather.2.cloned.1.call-start
  6.5 1.1 copy.13
  7.6 0.8 copy.14
  8.5 0.0 all-gather.2.cloned.1.call-update
  8.5 0.7 compare_select_fusion
  9.2 0.1 copy.15
  9.3 0.1 reshape.44
  9.4 0.0 copy-done
  9.4 0.6 gather_fusion
  10.0 0.1 reshape.43
  10.1 0.7 fusion.2
  25.9 35.6 %all-gather.2.cloned.1.call-done = bf16[16,512,128]{2,1,0:T(8,128)(2,1)} async-done(((bf16[2,512,128]{2,1,0:T(8,128)(2,1)}), bf16[16,512,128]{2,1,0:T(8,128)(2,1)}) %all-gather.2.cloned.1.call-update) | async-done | bytes 2097168 | tf_op jit(solution)/shard_map/all_gather | solution.py:159
  61.5 1.6 %dynamic-slice_dynamic-update-slice_fusion.7 = bf16[8,512,128]{2,1,0:T(8,128)(2,1)} fusion(bf16[16,512,128]{2,1,0:T(8,128)(2,1)} %all-gather.2.cloned.1.call-done, s32[]{:T(128)S(6)} %select_n.57), kind=kLoop, calls=%fused_computation.8 | loop fusion | bytes 262148
  63.1 1.6 %dynamic-slice_dynamic-update-slice_fusion.6 = bf16[8,512,128]{2,1,0:T(8,128)(2,1)} fusion(bf16[8,512,128]{2,1,0:T(8,128)(2,1)} %dynamic-slice_dynamic-update-slice_fusion.7, bf16[16,512,128]{2,1,0:T(8,128)(2,1)} %all-gather.2.cloned.1.call-done, s32[]{:T(128)S(6)} %select_n.58), kind=kLoop, calls=%fused_computation.7 | loop fusion | bytes 262148
  64.7 1.6 %dynamic-slice_dynamic-update-slice_fusion.5 = bf16[8,512,128]{2,1,0:T(8,128)(2,1)} fusion(bf16[8,512,128]{2,1,0:T(8,128)(2,1)} %dynamic-slice_dynamic-update-slice_fusion.6, bf16[16,512,128]{2,1,0:T(8,128)(2,1)} %all-gather.2.cloned.1.call-done, s32[]{:T(128)S(6)} %select_n.59), kind=kLoop, calls=%fused_computation.6 | loop fusion | bytes 262148
  66.2 1.6 %dynamic-slice_dynamic-update-slice_fusion.4 = bf16[8,512,128]{2,1,0:T(8,128)(2,1)} fusion(bf16[8,512,128]{2,1,0:T(8,128)(2,1)} %dynamic-slice_dynamic-update-slice_fusion.5, bf16[16,512,128]{2,1,0:T(8,128)(2,1)} %all-gather.2.cloned.1.call-done, s32[]{:T(128)S(6)} %select_n.60), kind=kLoop, calls=%fused_computation.5 | loop fusion | bytes 262148
  67.8 1.6 %dynamic-slice_dynamic-update-slice_fusion.3 = bf16[8,512,128]{2,1,0:T(8,128)(2,1)} fusion(bf16[8,512,128]{2,1,0:T(8,128)(2,1)} %dynamic-slice_dynamic-update-slice_fusion.4, bf16[16,512,128]{2,1,0:T(8,128)(2,1)} %all-gather.2.cloned.1.call-done, s32[]{:T(128)S(6)} %select_n.61), kind=kLoop, calls=%fused_computation.4 | loop fusion | bytes 262148
  69.3 1.6 %dynamic-slice_dynamic-update-slice_fusion.2 = bf16[8,512,128]{2,1,0:T(8,128)(2,1)} fusion(bf16[8,512,128]{2,1,0:T(8,128)(2,1)} %dynamic-slice_dynamic-update-slice_fusion.3, bf16[16,512,128]{2,1,0:T(8,128)(2,1)} %all-gather.2.cloned.1.call-done, s32[]{:T(128)S(6)} %select_n.62), kind=kLoop, calls=%fused_computation.3 | loop fusion | bytes 262148
  70.9 1.6 %dynamic-slice_dynamic-update-slice_fusion.1 = bf16[8,512,128]{2,1,0:T(8,128)(2,1)} fusion(bf16[8,512,128]{2,1,0:T(8,128)(2,1)} %dynamic-slice_dynamic-update-slice_fusion.2, bf16[16,512,128]{2,1,0:T(8,128)(2,1)} %all-gather.2.cloned.1.call-done, s32[]{:T(128)S(6)} %select_n.63), kind=kLoop, calls=%fused_computation.2 | loop fusion | bytes 262148
  72.5 1.6 %dynamic-slice_dynamic-update-slice_fusion = bf16[8,512,128]{2,1,0:T(8,128)(2,1)} fusion(bf16[8,512,128]{2,1,0:T(8,128)(2,1)} %dynamic-slice_dynamic-update-slice_fusion.1, bf16[16,512,128]{2,1,0:T(8,128)(2,1)} %all-gather.2.cloned.1.call-done, s32[]{:T(128)S(6)} %select_n.64), kind=kLoop, calls=%fused_computation.1 | loop fusion | bytes 262148 | tf_op jit(solution)/shard_map/stack | solution.py:165
  74.0 3.5 %all-to-all-start = ((bf16[4,2,512,128]{3,2,1,0:T(8,128)(2,1)}), bf16[4,2,512,128]{3,2,1,0:T(8,128)(2,1)S(1)}, u32[]{:S(2)}, u32[]{:S(2)}) async-start(bf16[4,2,512,128]{3,2,1,0:T(8,128)(2,1)} %bitcast.12), calls=%async_computation | async-start | bytes 2097152 | tf_op jit(solution)/shard_map/all_to_all | solution.py:166
  77.5 1.3 dynamic_slice.31
  79.5 12.5 %all-to-all-done = bf16[4,2,512,128]{3,2,1,0:T(8,128)(2,1)S(1)} async-done(((bf16[4,2,512,128]{3,2,1,0:T(8,128)(2,1)}), bf16[4,2,512,128]{3,2,1,0:T(8,128)(2,1)S(1)}, u32[]{:S(2)}, u32[]{:S(2)}) %all-to-all-start) | async-done | bytes 1048608 | tf_op jit(solution)/shard_map/all_to_all | solution.py:166
  92.0 0.1 fusion.1
  92.0 0.2 copy.17
  92.3 22.5 %shard_map.46 = f32[128,128]{1,0:T(8,128)S(1)} custom-call(bf16[128,2048]{1,0:T(8,128)(2,1)S(1)} %bitcast.23, bf16[2048,128]{1,0:T(8,128)(2,1)S(1)} %bitcast.24), custom_call_target="tpu_custom_call" | custom-call | tf_op jit(solution)/shard_map/pallas_call | solution.py:133
  114.8 6.5 %all_to_all.10 = f32[4,32,128]{2,1,0:T(8,128)S(1)} all-to-all(f32[4,32,128]{2,1,0:T(8,128)S(1)} %bitcast.27), channel_id=1, replica_groups=mesh['pair'=8,'cell'=4] {'cell'}, dimensions={0} | all-to-all | bytes 131072 | tf_op jit(solution)/shard_map/all_to_all | solution.py:173
  121.3 0.6 copy.26
  (2 shorter events, 0.0 us)
Async XLA Ops:
  6.5 2.9 %copy-start = (s32[16]{0:T(128)S(1)}, s32[16]{0:T(128)}, u32[]{:S(2)}) copy-start(s32[16]{0:T(128)} %param.5) | copy-start | bytes 196
  6.5 55.0 %all-gather.2.cloned.1.call-start = ((), (), s32[]{:S(2)}) async-start(), calls=%async_computation.2 | async-start | bytes 2359296 | tf_op jit(solution)/shard_map/all_gather | solution.py:159
  74.0 18.0 %all-to-all-start = ((bf16[4,2,512,128]{3,2,1,0:T(8,128)(2,1)}), bf16[4,2,512,128]{3,2,1,0:T(8,128)(2,1)S(1)}, u32[]{:S(2)}, u32[]{:S(2)}) async-start(bf16[4,2,512,128]{3,2,1,0:T(8,128)(2,1)} %bitcast.12), calls=%async_computation | async-start | bytes 2097152 | tf_op jit(solution)/shard_map/all_to_all | solution.py:166
Sparse Core Ops, SparseCore 0:
  9.5 52.0 all-gather.1

commit v2 on v1

--- a/solution.py
+++ b/solution.py
@@ -77,21 +77,196 @@
     return v * jnp.log(jnp.maximum(v, 1e-30))
 
 
-def kernel(first_ref, second_ref, out_ref, wf, ws, part, left):
-    cells = second_ref.shape[0]
+def grid_of(tables):
+    columns = 1
+    while 2 * (2 * columns) * (2 * columns) <= tables and tables % (2 * columns) == 0:
+        columns *= 2
+    return tables // columns, columns
+
+
+def route(tables, groups, pieces, wanted_ref, expr_ref, out_ref, *scratch):
+    gath = scratch[:pieces]
+    chosen, z_send, z_recv, x_send, x_recv, c_send, c_recv = scratch[pieces:]
+    zs, xs = grid_of(tables)
+    split = groups // ROUNDS
+    me = lax.axis_index("pair")
+    group = lax.axis_index("cell")
+    z = lax.div(me, xs)
+    x = lax.rem(me, xs)
+    rows = expr_ref.shape[0]
+    part = rows // pieces
+    mesh_id = pl.DeviceIdType.MESH
+
+    def own_pair(ch):
+        return gath[ch].at[pl.ds(2 * me, 2)]
+
+    def z_copy(ch, step, up, owner_z, to_z):
+        ref = gath[ch].at[pl.ds(2 * (owner_z * xs + x), 2)]
+        return pltpu.make_async_remote_copy(
+            src_ref=ref, dst_ref=ref,
+            send_sem=z_send.at[up, ch, step], recv_sem=z_recv.at[up, ch, step],
+            device_id=(to_z * xs + x, group), device_id_type=mesh_id,
+        )
+
+    def up_out(ch, step):
+        return (z + 1 < zs) & (z - step + 1 >= 0), z_copy(ch, step, 1, z - step + 1, z + 1)
+
+    def down_out(ch, step):
+        return (z >= 1) & (z + step - 1 < zs), z_copy(ch, step, 0, z + step - 1, z - 1)
+
+    def up_in(ch, step):
+        return z - step >= 0, z_copy(ch, step, 1, z - step, z - 1)
+
+    def down_in(ch, step):
+        return z + step < zs, z_copy(ch, step, 0, z + step, z + 1)
+
+    def x_copy(ch, owner_z, owner_x, d):
+        ref = gath[ch].at[pl.ds(2 * (owner_z * xs + owner_x), 2)]
+        return pltpu.make_async_remote_copy(
+            src_ref=ref, dst_ref=ref,
+            send_sem=x_send.at[ch, owner_z, d], recv_sem=x_recv.at[ch, owner_z, d],
+            device_id=(z * xs + lax.rem(x + d, xs), group), device_id_type=mesh_id,
+        )
+
+    def c_copy(ch, d):
+        to = lax.rem(group + d, groups)
+        return pltpu.make_async_remote_copy(
+            src_ref=chosen.at[ch, to],
+            dst_ref=out_ref.at[:, pl.ds(pl.multiple_of(group * rows + ch * part, part), part)],
+            send_sem=c_send.at[ch, d], recv_sem=c_recv.at[ch, d],
+            device_id=(me, to), device_id_type=mesh_id,
+        )
+
+    def share_row(ch, owner_z):
+        for d in range(1, xs):
+            x_copy(ch, owner_z, x, d).start()
+
+    barrier = pltpu.get_barrier_semaphore()
+
+    @pl.when(z >= 1)
+    def _():
+        pl.semaphore_signal(barrier, inc=1, device_id=(me - xs, group), device_id_type=mesh_id)
+
+    @pl.when(z + 1 < zs)
+    def _():
+        pl.semaphore_signal(barrier, inc=1, device_id=(me + xs, group), device_id_type=mesh_id)
+
+    for d in range(1, xs):
+        pl.semaphore_signal(
+            barrier, inc=1, device_id=(z * xs + lax.rem(x + d, xs), group), device_id_type=mesh_id
+        )
+    for d in range(1, groups):
+        pl.semaphore_signal(
+            barrier, inc=1, device_id=(me, lax.rem(group + d, groups)), device_id_type=mesh_id
+        )
+    for ch in range(pieces):
+        for h in range(2):
+            gath[ch][2 * me + h] = expr_ref[ch * part:(ch + 1) * part, h * BLOCK:(h + 1) * BLOCK]
+    z_peers = lax.div(z + zs - 1, zs) + lax.div(2 * zs - 2 - z, zs)
+    pl.semaphore_wait(barrier, xs + groups - 2 + z_peers)
+
+    def begin(copy_if):
+        cond, copy = copy_if
+
+        @pl.when(cond)
+        def _():
+            copy.start()
+
+    def advance(ch, step):
+        if step == 0:
+            begin(up_out(ch, 1))
+            begin(down_out(ch, 1))
+            share_row(ch, z)
+            return
+        for arrive, leave, owner in ((up_in, up_out, z - step), (down_in, down_out, z + step)):
+            cond, copy = arrive(ch, step)
+
+            @pl.when(cond)
+            def _():
+                copy.wait_recv()
+                if step + 1 < zs:
+                    begin(leave(ch, step + 1))
+                share_row(ch, owner)
+
+    def choose(ch):
+        for owner_z in range(zs):
+            for d in range(1, xs):
+                x_copy(ch, owner_z, lax.rem(x + xs - d, xs), d).wait_recv()
+        for c in range(groups):
+            for s in range(2):
+                chosen[ch, c, s] = gath[ch][wanted_ref[2 * (c // split) + s]]
+        for d in range(1, groups):
+            c_copy(ch, d).start()
+        out_ref[:, pl.ds(pl.multiple_of(group * rows + ch * part, part), part)] = chosen[ch, group]
+
+    for tick in range(pieces + zs - 1):
+        for ch in range(pieces):
+            if 0 <= tick - ch < zs:
+                advance(ch, tick - ch)
+        if tick >= zs - 1:
+            choose(tick - zs + 1)
+
+    for ch in range(pieces):
+        for d in range(1, groups):
+            c_copy(ch, d).wait_send()
+            c_copy(ch, d).wait_recv()
+        for step in range(1, zs):
+            for cond, copy in (up_out(ch, step), down_out(ch, step)):
+
+                @pl.when(cond)
+                def _():
+                    copy.wait_send()
+        for owner_z in range(zs):
+            for d in range(1, xs):
+                x_copy(ch, owner_z, x, d).wait_send()
+
+
+def seat_blocks(expression, wanted, tables, groups):
+    rows = expression.shape[0]
+    zs, xs = grid_of(tables)
+    pieces = 4
+    part = rows // pieces
+    dma = pltpu.SemaphoreType.DMA
+    return pl.pallas_call(
+        functools.partial(route, tables, groups, pieces),
+        out_shape=jax.ShapeDtypeStruct((2, rows * groups, BLOCK), jnp.bfloat16),
+        in_specs=[
+            pl.BlockSpec(memory_space=pltpu.SMEM),
+            pl.BlockSpec(memory_space=pltpu.VMEM),
+        ],
+        out_specs=pl.BlockSpec(memory_space=pltpu.VMEM),
+        scratch_shapes=[pltpu.VMEM((2 * tables, part, BLOCK), jnp.bfloat16)] * pieces
+        + [
+            pltpu.VMEM((pieces, groups, 2, part, BLOCK), jnp.bfloat16),
+            dma((2, pieces, zs)),
+            dma((2, pieces, zs)),
+            dma((pieces, zs, xs)),
+            dma((pieces, zs, xs)),
+            dma((pieces, groups)),
+            dma((pieces, groups)),
+        ],
+        compiler_params=pltpu.CompilerParams(
+            collective_id=0, has_side_effects=True, vmem_limit_bytes=40 * 1024 * 1024
+        ),
+    )(wanted, expression)
+
+
+def kernel(x_ref, out_ref, wf, ws, part, left):
+    cells = x_ref.shape[1]
 
     @pl.loop(0, cells // 128)
     def _(c):
         at = pl.ds(pl.multiple_of(c * 128, 128), 128)
+        turned = x_ref[0, at, :].astype(jnp.float32).T
         for g in range(0, 128, 32):
-            vals = basis(first_ref[g:g + 32, at], 1.0)
+            vals = basis(turned[g:g + 32], 1.0)
             for i in range(BINS):
                 wf[i * BLOCK + g:i * BLOCK + g + 32, at] = vals[i].astype(jnp.bfloat16)
 
     @pl.loop(0, cells // 32)
     def _(c):
         at = pl.ds(pl.multiple_of(c * 32, 32), 32)
-        vals = basis(second_ref[at, :], 1.0 / cells)
+        vals = basis(x_ref[1, at, :], 1.0 / cells)
         for i in range(BINS):
             ws[at, i * BLOCK:(i + 1) * BLOCK] = vals[i].astype(jnp.bfloat16)
 
@@ -128,12 +303,12 @@
         out_ref[pl.ds(base, 16), :] = total
 
 
-def pair_information(first, second):
-    cells = second.shape[0]
+def pair_information(blocks):
+    cells = blocks.shape[1]
     return pl.pallas_call(
         kernel,
         out_shape=jax.ShapeDtypeStruct((BLOCK, BLOCK), jnp.float32),
-        in_specs=[pl.BlockSpec(memory_space=pltpu.VMEM)] * 2,
+        in_specs=[pl.BlockSpec(memory_space=pltpu.VMEM)],
         out_specs=pl.BlockSpec(memory_space=pltpu.VMEM),
         scratch_shapes=[
             pltpu.VMEM((BINS * BLOCK, cells), jnp.bfloat16),
@@ -142,7 +317,7 @@
             pltpu.VMEM((BINS * BLOCK, BLOCK), jnp.float32),
         ],
         compiler_params=pltpu.CompilerParams(vmem_limit_bytes=48 * 1024 * 1024),
-    )(first, second)
+    )(blocks)
 
 
 def local(expression, plan, screen):
@@ -151,22 +326,9 @@
     split = groups // ROUNDS
     table = lax.axis_index("pair")
     group = lax.axis_index("cell")
-    rows = expression.shape[0]
-    cells = rows * groups
     seats = jnp.asarray(seat_table(tables))[table]
-    wanted = plan[seats]
-    blocks = expression.reshape(rows, 2, BLOCK).transpose(1, 0, 2)
-    blocks = lax.all_gather(blocks, "pair", axis=0, tiled=True)
-    order = [r // split for r in range(groups)]
-    parts = []
-    for c in range(groups):
-        for s in range(2):
-            parts.append(lax.dynamic_index_in_dim(blocks, wanted[order[c], s], 0, keepdims=False))
-    send = jnp.stack(parts).reshape(groups, 2, rows, BLOCK)
-    got = lax.all_to_all(send, "cell", 0, 0, tiled=True)
-    first = got[:, 0].reshape(cells, BLOCK).T
-    second = got[:, 1].reshape(cells, BLOCK)
-    mine = pair_information(first, second)
+    wanted = plan[seats].reshape(2 * ROUNDS)
+    mine = pair_information(seat_blocks(expression, wanted, tables, groups))
     mine = jnp.where(screen[group // split, table] == 1, mine, jnp.float32(0.0))
     share = BLOCK // groups
     if split == 1:

time: 129 us -> 72.9 us (0.57)
  waiting for transfers between devices: 48.2 us -> 0 us
  Pallas kernels: 22.5 us -> 61.6 us
  between operations: 29.2 us -> 0.69 us
  local copies, waits for them, and re-layouts: 18.2 us -> 3.03 us
  starting transfers between devices: 3.52 us -> 0 us
    pallas_call x0 -> x1, Pallas kernels: none -> 37.7 us  [seat_blocks(): pl.pallas_call(functools.partial(route, tables, groups, pieces), out_shap...]
    all_gather x1 -> x0, waiting for transfers between devices: 35.6 us -> none  [local(): blocks = lax.all_gather(blocks, 'pair', axis=0, tiled=True)]
    all_to_all x1 -> x0, waiting for transfers between devices: 12.5 us -> none  [local(): got = lax.all_to_all(send, 'cell', 0, 0, tiled=True)]
    unnamed x11 -> x5, local copies, waits for them, and re-layouts: 12.6 us -> 0.94 us
    all_to_all x1 -> x0, starting transfers between devices: 3.51 us -> none  [local(): got = lax.all_to_all(send, 'cell', 0, 0, tiled=True)]
    another operation x2 -> x0, local copies, waits for them, and re-layouts: 1.79 us -> none  [the longest x1 1.56 us: local(): send = jnp.stack(parts).reshape(groups, 2, rows, BLOCK)]
    pallas_call x1, Pallas kernels: 22.5 us -> 23.9 us  [pair_information(): pl.pallas_call(kernel, out_shape=jax.ShapeDtypeStruct((BLOCK, BLOCK), jnp...]
  transfers between devices with their start and end apart: 2 -> 0, of which waited for: 2 -> 0; matrix products, arithmetic and copies ran while one was open for 3% -> 0% of each run, Pallas kernels for 0% -> 0%
where the time goes in v2:
time: 72.9 us; the launch traced here: 72.7 us
  Pallas kernels  61.6 us (84%)
  blocking collectives  6.68 us (9%)
  local copies, waits for them, and re-layouts  3.03 us (4%)
    pallas_call x1, Pallas kernels, seat_blocks(): pl.pallas_call(functools.partial(route, tables, groups, pieces), out_shap...  37.7 us
    pallas_call x1, Pallas kernels, pair_information(): pl.pallas_call(kernel, out_shape=jax.ShapeDtypeStruct((BLOCK, BLOCK), jnp...  23.9 us
    all_to_all x1, blocking collectives, local(): lax.all_to_all(mine.reshape(groups, share, BLOCK), 'cell', 0, 0, tiled=True)  6.68 us

profile of v2, /device:TPU:0, one launch (start us, length us, event | category | flops | bytes accessed | tf_op | source)
XLA Modules:
  0.0 72.7 jit_solution(13114798563924867401)
XLA Ops:
  0.0 0.0 copy-start
  0.0 0.7 compare_select_fusion
  0.7 0.1 copy.6
  0.8 0.1 reshape.40
  0.9 0.0 copy-done
  0.9 0.0 copy-start.1
  0.9 0.6 gather_fusion
  1.5 0.3 copy-done.1
  1.8 37.7 %shard_map.46.x_ref = bf16[2,2048,128]{2,1,0:T(8,128)(2,1)S(1)} custom-call(s32[8]{0:T(128)S(1)} %gather_fusion, bf16[512,256]{1,0:T(8,128)(2,1)S(1)} %copy-done.1), custom_call_target="tpu_custom_call" | custom-call | tf_op jit(solution)/shard_map/pallas_call | solution.py:230
  39.5 23.9 %shard_map.47 = f32[128,128]{1,0:T(8,128)S(1)} custom-call(bf16[2,2048,128]{2,1,0:T(8,128)(2,1)S(1)} %shard_map.46.x_ref), custom_call_target="tpu_custom_call" | custom-call | tf_op jit(solution)/shard_map/pallas_call | solution.py:308
  63.4 1.3 %dynamic_slice.6 = s32[1,1]{1,0:T(1,128)} dynamic-slice(s32[4,8]{1,0:T(4,128)} %param.6, s32[]{:T(128)S(6)} %select_n.28, s32[]{:T(128)S(6)} %select_n.29), dynamic_slice_sizes={1,1} | dynamic-slice | bytes 12 | tf_op jit(solution)/shard_map/dynamic_slice | solution.py:332
  65.4 6.7 %all_to_all.5 = f32[4,32,128]{2,1,0:T(8,128)S(1)} all-to-all(f32[4,32,128]{2,1,0:T(8,128)S(1)} %bitcast.6), channel_id=1, replica_groups=mesh['pair'=8,'cell'=4] {'cell'}, dimensions={0} | all-to-all | bytes 131072 | tf_op jit(solution)/shard_map/all_to_all | solution.py:335
  72.0 0.6 copy.8
  (2 shorter events, 0.0 us)
Async XLA Ops:
  0.0 0.9 %copy-start = (s32[16]{0:T(128)S(1)}, s32[16]{0:T(128)}, u32[]{:S(2)}) copy-start(s32[16]{0:T(128)} %param.5) | copy-start | bytes 196
  0.9 1.0 %copy-start.1 = (bf16[512,256]{1,0:T(8,128)(2,1)S(1)}, bf16[512,256]{1,0:T(8,128)(2,1)}, u32[]{:S(2)}) copy-start(bf16[512,256]{1,0:T(8,128)(2,1)} %expr_ref.1) | copy-start | bytes 786436

commit v3 on v2

--- a/solution.py
+++ b/solution.py
@@ -2,7 +2,6 @@
 
 import jax
 import jax.numpy as jnp
-import numpy as np
 from jax import lax
 from jax.experimental import pallas as pl
 from jax.experimental.pallas import tpu as pltpu
@@ -13,16 +12,16 @@
 ROUNDS = 4
 
 
-def seat_table(tables):
-    firsts = [2 * p for p in range(tables)]
-    seconds = [2 * p + 1 for p in range(tables)]
-    out = np.zeros((tables, ROUNDS, 2), np.int32)
-    for r in range(ROUNDS):
-        if r > 0:
-            firsts, seconds = firsts[:1] + seconds[:1] + firsts[1:-1], seconds[1:] + firsts[-1:]
-        out[:, r, 0] = firsts
-        out[:, r, 1] = seconds
-    return out
+def seat_of(tables, table, turn):
+    ring = 2 * tables - 1
+
+    def start(place):
+        was = lax.rem(place + ring - turn, ring)
+        other = 2 * lax.rem(ring - was, ring) + 1
+        return jnp.where((was >= 1) & (was < tables), 2 * was, other)
+
+    first = jnp.where(table == 0, 0, start(table))
+    return first, start(lax.rem(ring - table, ring))
 
 
 def basis(x, scale):
@@ -84,9 +83,10 @@
     return tables // columns, columns
 
 
-def route(tables, groups, pieces, wanted_ref, expr_ref, out_ref, *scratch):
+def kernel(tables, groups, pieces, plan_ref, expr_ref, out_ref, *scratch):
     gath = scratch[:pieces]
-    chosen, z_send, z_recv, x_send, x_recv, c_send, c_recv = scratch[pieces:]
+    chosen, seated, wf, ws, part_sums, left, mine = scratch[pieces:pieces + 7]
+    z_send, z_recv, x_send, x_recv, c_send, c_recv, o_send, o_recv = scratch[pieces + 7:]
     zs, xs = grid_of(tables)
     split = groups // ROUNDS
     me = lax.axis_index("pair")
@@ -132,7 +132,7 @@
         to = lax.rem(group + d, groups)
         return pltpu.make_async_remote_copy(
             src_ref=chosen.at[ch, to],
-            dst_ref=out_ref.at[:, pl.ds(pl.multiple_of(group * rows + ch * part, part), part)],
+            dst_ref=seated.at[:, pl.ds(pl.multiple_of(group * rows + ch * part, part), part)],
             send_sem=c_send.at[ch, d], recv_sem=c_recv.at[ch, d],
             device_id=(me, to), device_id_type=mesh_id,
         )
@@ -193,23 +193,90 @@
             for d in range(1, xs):
                 x_copy(ch, owner_z, lax.rem(x + xs - d, xs), d).wait_recv()
         for c in range(groups):
-            for s in range(2):
-                chosen[ch, c, s] = gath[ch][wanted_ref[2 * (c // split) + s]]
+            for s, seat in enumerate(seat_of(tables, me, c // split)):
+                chosen[ch, c, s] = gath[ch][plan_ref[seat]]
         for d in range(1, groups):
             c_copy(ch, d).start()
-        out_ref[:, pl.ds(pl.multiple_of(group * rows + ch * part, part), part)] = chosen[ch, group]
-
-    for tick in range(pieces + zs - 1):
+        seated[:, pl.ds(pl.multiple_of(group * rows + ch * part, part), part)] = chosen[ch, group]
+
+    def weigh(ch):
+        for d in range(1, groups):
+            c_copy(ch, d).wait_recv()
+
+        @pl.loop(0, groups)
+        def _(g):
+            base = pl.multiple_of(g * rows + ch * part, part)
+            at = pl.ds(base, part)
+            turned = seated[0, at, :].astype(jnp.float32).T
+            for k in range(0, BLOCK, 32):
+                vals = basis(turned[k:k + 32], 1.0)
+                for i in range(BINS):
+                    wf[i * BLOCK + k:i * BLOCK + k + 32, at] = vals[i].astype(jnp.bfloat16)
+            for k in range(0, part, 32):
+                rows_at = pl.ds(base + k, 32)
+                vals = basis(seated[1, rows_at, :], 1.0 / (rows * groups))
+                for i in range(BINS):
+                    ws[rows_at, i * BLOCK:(i + 1) * BLOCK] = vals[i].astype(jnp.bfloat16)
+
+    for tick in range(pieces + zs + 1):
         for ch in range(pieces):
             if 0 <= tick - ch < zs:
                 advance(ch, tick - ch)
-        if tick >= zs - 1:
-            choose(tick - zs + 1)
-
+        if 0 <= tick - zs < pieces:
+            choose(tick - zs)
+        if 0 <= tick - zs - 1 < pieces:
+            weigh(tick - zs - 1)
+
+    mine[...] = jnp.zeros_like(mine)
+    left[...] = jnp.zeros_like(left)
+    for j in range(BINS // 2):
+        part_sums[...] = jnp.dot(
+            wf[...], ws[:, j * 2 * BLOCK:(j + 1) * 2 * BLOCK], preferred_element_type=jnp.float32
+        )
+
+        @pl.loop(0, BLOCK // 16)
+        def _(g):
+            base = pl.multiple_of(g * 16, 16)
+            total = mine[pl.ds(base, 16), :]
+            right0 = jnp.zeros((16, BLOCK), jnp.float32)
+            right1 = right0
+            for i in range(BINS):
+                rows = pl.ds(i * BLOCK + base, 16)
+                v0 = part_sums[rows, :BLOCK]
+                v1 = part_sums[rows, BLOCK:]
+                total += entropy_terms(v0) + entropy_terms(v1)
+                right0 += v0
+                right1 += v1
+                left[rows, :] += v0 + v1
+            total -= entropy_terms(right0) + entropy_terms(right1)
+            mine[pl.ds(base, 16), :] = total
+
+    @pl.loop(0, BLOCK // 16)
+    def _(g):
+        base = pl.multiple_of(g * 16, 16)
+        total = mine[pl.ds(base, 16), :]
+        for i in range(BINS):
+            total -= entropy_terms(left[pl.ds(i * BLOCK + base, 16), :])
+        mine[pl.ds(base, 16), :] = total
+
+    share = out_ref.shape[1]
+    turn = lax.div(group, split)
+
+    def o_copy(k):
+        to = lax.rem(group + k * split, groups)
+        return pltpu.make_async_remote_copy(
+            src_ref=mine.at[pl.ds(pl.multiple_of(to * share, share), share)],
+            dst_ref=out_ref.at[turn],
+            send_sem=o_send.at[k], recv_sem=o_recv.at[k],
+            device_id=(me, to), device_id_type=mesh_id,
+        )
+
+    for k in range(1, ROUNDS):
+        o_copy(k).start()
+    out_ref[turn] = mine[pl.ds(pl.multiple_of(group * share, share), share), :]
     for ch in range(pieces):
         for d in range(1, groups):
             c_copy(ch, d).wait_send()
-            c_copy(ch, d).wait_recv()
         for step in range(1, zs):
             for cond, copy in (up_out(ch, step), down_out(ch, step)):
 
@@ -219,17 +286,22 @@
         for owner_z in range(zs):
             for d in range(1, xs):
                 x_copy(ch, owner_z, x, d).wait_send()
-
-
-def seat_blocks(expression, wanted, tables, groups):
+    for k in range(1, ROUNDS):
+        o_copy(k).wait()
+
+
+def local(expression, plan, screen):
+    tables = lax.axis_size("pair")
+    groups = lax.axis_size("cell")
     rows = expression.shape[0]
+    cells = rows * groups
     zs, xs = grid_of(tables)
-    pieces = 4
+    pieces = rows // BLOCK
     part = rows // pieces
     dma = pltpu.SemaphoreType.DMA
-    return pl.pallas_call(
-        functools.partial(route, tables, groups, pieces),
-        out_shape=jax.ShapeDtypeStruct((2, rows * groups, BLOCK), jnp.bfloat16),
+    values = pl.pallas_call(
+        functools.partial(kernel, tables, groups, pieces),
+        out_shape=jax.ShapeDtypeStruct((ROUNDS, BLOCK // groups, BLOCK), jnp.float32),
         in_specs=[
             pl.BlockSpec(memory_space=pltpu.SMEM),
             pl.BlockSpec(memory_space=pltpu.VMEM),
@@ -238,103 +310,27 @@
         scratch_shapes=[pltpu.VMEM((2 * tables, part, BLOCK), jnp.bfloat16)] * pieces
         + [
             pltpu.VMEM((pieces, groups, 2, part, BLOCK), jnp.bfloat16),
+            pltpu.VMEM((2, cells, BLOCK), jnp.bfloat16),
+            pltpu.VMEM((BINS * BLOCK, cells), jnp.bfloat16),
+            pltpu.VMEM((cells, BINS * BLOCK), jnp.bfloat16),
+            pltpu.VMEM((BINS * BLOCK, 2 * BLOCK), jnp.float32),
+            pltpu.VMEM((BINS * BLOCK, BLOCK), jnp.float32),
+            pltpu.VMEM((BLOCK, BLOCK), jnp.float32),
             dma((2, pieces, zs)),
             dma((2, pieces, zs)),
             dma((pieces, zs, xs)),
             dma((pieces, zs, xs)),
             dma((pieces, groups)),
             dma((pieces, groups)),
+            dma((ROUNDS,)),
+            dma((ROUNDS,)),
         ],
         compiler_params=pltpu.CompilerParams(
-            collective_id=0, has_side_effects=True, vmem_limit_bytes=40 * 1024 * 1024
+            collective_id=0, has_side_effects=True, vmem_limit_bytes=52 * 1024 * 1024
         ),
-    )(wanted, expression)
-
-
-def kernel(x_ref, out_ref, wf, ws, part, left):
-    cells = x_ref.shape[1]
-
-    @pl.loop(0, cells // 128)
-    def _(c):
-        at = pl.ds(pl.multiple_of(c * 128, 128), 128)
-        turned = x_ref[0, at, :].astype(jnp.float32).T
-        for g in range(0, 128, 32):
-            vals = basis(turned[g:g + 32], 1.0)
-            for i in range(BINS):
-                wf[i * BLOCK + g:i * BLOCK + g + 32, at] = vals[i].astype(jnp.bfloat16)
-
-    @pl.loop(0, cells // 32)
-    def _(c):
-        at = pl.ds(pl.multiple_of(c * 32, 32), 32)
-        vals = basis(x_ref[1, at, :], 1.0 / cells)
-        for i in range(BINS):
-            ws[at, i * BLOCK:(i + 1) * BLOCK] = vals[i].astype(jnp.bfloat16)
-
-    out_ref[...] = jnp.zeros_like(out_ref)
-    left[...] = jnp.zeros_like(left)
-    for j in range(BINS // 2):
-        part[...] = jnp.dot(
-            wf[...], ws[:, j * 2 * BLOCK:(j + 1) * 2 * BLOCK], preferred_element_type=jnp.float32
-        )
-
-        @pl.loop(0, BLOCK // 16)
-        def _(g):
-            base = pl.multiple_of(g * 16, 16)
-            total = out_ref[pl.ds(base, 16), :]
-            right0 = jnp.zeros((16, BLOCK), jnp.float32)
-            right1 = right0
-            for i in range(BINS):
-                rows = pl.ds(i * BLOCK + base, 16)
-                v0 = part[rows, :BLOCK]
-                v1 = part[rows, BLOCK:]
-                total += entropy_terms(v0) + entropy_terms(v1)
-                right0 += v0
-                right1 += v1
-                left[rows, :] += v0 + v1
-            total -= entropy_terms(right0) + entropy_terms(right1)
-            out_ref[pl.ds(base, 16), :] = total
-
-    @pl.loop(0, BLOCK // 16)
-    def _(g):
-        base = pl.multiple_of(g * 16, 16)
-        total = out_ref[pl.ds(base, 16), :]
-        for i in range(BINS):
-            total -= entropy_terms(left[pl.ds(i * BLOCK + base, 16), :])
-        out_ref[pl.ds(base, 16), :] = total
-
-
-def pair_information(blocks):
-    cells = blocks.shape[1]
-    return pl.pallas_call(
-        kernel,
-        out_shape=jax.ShapeDtypeStruct((BLOCK, BLOCK), jnp.float32),
-        in_specs=[pl.BlockSpec(memory_space=pltpu.VMEM)],
-        out_specs=pl.BlockSpec(memory_space=pltpu.VMEM),
-        scratch_shapes=[
-            pltpu.VMEM((BINS * BLOCK, cells), jnp.bfloat16),
-            pltpu.VMEM((cells, BINS * BLOCK), jnp.bfloat16),
-            pltpu.VMEM((BINS * BLOCK, 2 * BLOCK), jnp.float32),
-            pltpu.VMEM((BINS * BLOCK, BLOCK), jnp.float32),
-        ],
-        compiler_params=pltpu.CompilerParams(vmem_limit_bytes=48 * 1024 * 1024),
-    )(blocks)
-
-
-def local(expression, plan, screen):
-    tables = lax.axis_size("pair")
-    groups = lax.axis_size("cell")
-    split = groups // ROUNDS
-    table = lax.axis_index("pair")
-    group = lax.axis_index("cell")
-    seats = jnp.asarray(seat_table(tables))[table]
-    wanted = plan[seats].reshape(2 * ROUNDS)
-    mine = pair_information(seat_blocks(expression, wanted, tables, groups))
-    mine = jnp.where(screen[group // split, table] == 1, mine, jnp.float32(0.0))
-    share = BLOCK // groups
-    if split == 1:
-        return lax.all_to_all(mine.reshape(groups, share, BLOCK), "cell", 0, 0, tiled=True)
-    every = lax.all_gather(mine, "cell", axis=0)[::split]
-    return lax.dynamic_slice_in_dim(every, group * share, share, 1)
+    )(plan, expression)
+    passed = lax.dynamic_slice_in_dim(screen, lax.axis_index("pair"), 1, 1)
+    return jnp.where(passed[:, :, None] == 1, values, jnp.float32(0.0))
 
 
 def solution(mesh):

time: 72.9 us -> 62.1 us (0.85)
  blocking collectives: 6.68 us -> 0 us
  Pallas kernels: 61.6 us -> 58.9 us
  local copies, waits for them, and re-layouts: 3.03 us -> 2.1 us
    all_to_all x1 -> x0, blocking collectives: 6.68 us -> none  [local(): lax.all_to_all(mine.reshape(groups, share, BLOCK), 'cell', 0, 0, tiled=True)]
    pallas_call x2 -> x1, Pallas kernels: 61.6 us -> 58.9 us  [local(): pl.pallas_call(functools.partial(kernel, tables, groups, pieces), out_sha...]
    dynamic_slice x1 -> x0, local copies, waits for them, and re-layouts: 1.27 us -> none  [local(): mine = jnp.where(screen[group // split, table] == 1, mine, jnp.float32(0.0))]
    unnamed x5 -> x6, local copies, waits for them, and re-layouts: 0.94 us -> 2.1 us
where the time goes in v3:
time: 62.1 us; the launch traced here: 61.9 us
  Pallas kernels  58.9 us (95%)
  local copies, waits for them, and re-layouts  2.1 us (3%)
  other arithmetic  0.89 us (1%)
    pallas_call x1, Pallas kernels, local(): pl.pallas_call(functools.partial(kernel, tables, groups, pieces), out_sha...  58.9 us
    unnamed x6, local copies, waits for them, and re-layouts  2.1 us

profile of v3, /device:TPU:0, one launch (start us, length us, event | category | flops | bytes accessed | tf_op | source)
XLA Modules:
  0.0 61.9 jit_solution(8011987437443198858)
XLA Ops:
  0.0 0.0 copy-start.2
  0.0 0.7 %copy-done.2 = s32[4,8]{1,0:T(4,128)S(1)} copy-done((s32[4,8]{1,0:T(4,128)S(1)}, s32[4,8]{1,0:T(4,128)}, u32[]{:S(2)}) %copy-start.2) | copy-done | bytes 152
  0.7 0.0 copy-start.1
  0.7 0.2 fusion
  0.9 0.5 copy-done.1
  1.3 0.0 copy-start
  1.3 0.9 %copy-done = bf16[512,256]{1,0:T(8,128)(2,1)S(1)} copy-done((bf16[512,256]{1,0:T(8,128)(2,1)S(1)}, bf16[512,256]{1,0:T(8,128)(2,1)}, u32[]{:S(2)}) %copy-start) | copy-done | bytes 262168
  2.3 58.9 %shard_map.37 = f32[4,32,128]{2,1,0:T(8,128)S(1)} custom-call(s32[16]{0:T(128)S(1)} %copy-done.1, bf16[512,256]{1,0:T(8,128)(2,1)S(1)} %copy-done), custom_call_target="tpu_custom_call" | custom-call | tf_op jit(solution)/shard_map/pallas_call | solution.py:302
  61.2 0.7 %broadcast_select_fusion = f32[4,32,128]{2,1,0:T(8,128)} fusion(f32[4,32,128]{2,1,0:T(8,128)S(1)} %shard_map.37, pred[4]{0:T(512)(128)(4,1)S(1)} %fusion), kind=kLoop, calls=%fused_computation | loop fusion | flops 16384 | bytes 131076 | tf_op jit(solution)/shard_map/jit(_where)/select_n | solution.py:333
Async XLA Ops:
  0.0 0.7 %copy-start.2 = (s32[4,8]{1,0:T(4,128)S(1)}, s32[4,8]{1,0:T(4,128)}, u32[]{:S(2)}) copy-start(s32[4,8]{1,0:T(4,128)} %param.5) | copy-start | bytes 388
  0.7 0.7 %copy-start.1 = (s32[16]{0:T(128)S(1)}, s32[16]{0:T(128)}, u32[]{:S(2)}) copy-start(s32[16]{0:T(128)} %plan_ref.1) | copy-start | bytes 196
  1.3 0.9 %copy-start = (bf16[512,256]{1,0:T(8,128)(2,1)S(1)}, bf16[512,256]{1,0:T(8,128)(2,1)}, u32[]{:S(2)}) copy-start(bf16[512,256]{1,0:T(8,128)(2,1)} %expr_ref.1) | copy-start | bytes 786436

commit v4 on v3

--- a/solution.py
+++ b/solution.py
@@ -227,37 +227,41 @@
         if 0 <= tick - zs - 1 < pieces:
             weigh(tick - zs - 1)
 
-    mine[...] = jnp.zeros_like(mine)
-    left[...] = jnp.zeros_like(left)
-    for j in range(BINS // 2):
-        part_sums[...] = jnp.dot(
+    def multiply(j):
+        part_sums[j % 2] = jnp.dot(
             wf[...], ws[:, j * 2 * BLOCK:(j + 1) * 2 * BLOCK], preferred_element_type=jnp.float32
         )
 
-        @pl.loop(0, BLOCK // 16)
-        def _(g):
-            base = pl.multiple_of(g * 16, 16)
-            total = mine[pl.ds(base, 16), :]
-            right0 = jnp.zeros((16, BLOCK), jnp.float32)
-            right1 = right0
+    def fold(j):
+        sums = part_sums.at[j % 2]
+        for g in range(0, BLOCK, 16):
+            total = jnp.zeros((16, BLOCK), jnp.float32)
+            right0 = total
+            right1 = total
             for i in range(BINS):
-                rows = pl.ds(i * BLOCK + base, 16)
-                v0 = part_sums[rows, :BLOCK]
-                v1 = part_sums[rows, BLOCK:]
+                at = i * BLOCK + g
+                v0 = sums[at:at + 16, :BLOCK]
+                v1 = sums[at:at + 16, BLOCK:]
                 total += entropy_terms(v0) + entropy_terms(v1)
                 right0 += v0
                 right1 += v1
-                left[rows, :] += v0 + v1
+                if j == 0:
+                    left[at:at + 16, :] = v0 + v1
+                elif j + 1 < BINS // 2:
+                    left[at:at + 16, :] += v0 + v1
+                else:
+                    total -= entropy_terms(left[at:at + 16, :] + v0 + v1)
             total -= entropy_terms(right0) + entropy_terms(right1)
-            mine[pl.ds(base, 16), :] = total
-
-    @pl.loop(0, BLOCK // 16)
-    def _(g):
-        base = pl.multiple_of(g * 16, 16)
-        total = mine[pl.ds(base, 16), :]
-        for i in range(BINS):
-            total -= entropy_terms(left[pl.ds(i * BLOCK + base, 16), :])
-        mine[pl.ds(base, 16), :] = total
+            if j == 0:
+                mine[g:g + 16, :] = total
+            else:
+                mine[g:g + 16, :] += total
+
+    multiply(0)
+    for j in range(BINS // 2):
+        if j + 1 < BINS // 2:
+            multiply(j + 1)
+        fold(j)
 
     share = out_ref.shape[1]
     turn = lax.div(group, split)
@@ -313,7 +317,7 @@
             pltpu.VMEM((2, cells, BLOCK), jnp.bfloat16),
             pltpu.VMEM((BINS * BLOCK, cells), jnp.bfloat16),
             pltpu.VMEM((cells, BINS * BLOCK), jnp.bfloat16),
-            pltpu.VMEM((BINS * BLOCK, 2 * BLOCK), jnp.float32),
+            pltpu.VMEM((2, BINS * BLOCK, 2 * BLOCK), jnp.float32),
             pltpu.VMEM((BINS * BLOCK, BLOCK), jnp.float32),
             pltpu.VMEM((BLOCK, BLOCK), jnp.float32),
             dma((2, pieces, zs)),

time: 62.1 us -> 54.9 us (0.88)
  Pallas kernels: 58.9 us -> 51.7 us
    pallas_call x1, Pallas kernels: 58.9 us -> 51.7 us  [local(): pl.pallas_call(functools.partial(kernel, tables, groups, pieces), out_sha...]
where the time goes in v4:
time: 54.9 us; the launch traced here: 54.7 us
  Pallas kernels  51.7 us (94%)
  local copies, waits for them, and re-layouts  2.1 us (4%)
  other arithmetic  0.89 us (2%)
    pallas_call x1, Pallas kernels, local(): pl.pallas_call(functools.partial(kernel, tables, groups, pieces), out_sha...  51.7 us
    unnamed x6, local copies, waits for them, and re-layouts  2.1 us

profile of v4, /device:TPU:0, one launch (start us, length us, event | category | flops | bytes accessed | tf_op | source)
XLA Modules:
  0.0 54.7 jit_solution(10196407909499381144)
XLA Ops:
  0.0 0.0 copy-start.2
  0.0 0.7 %copy-done.2 = s32[4,8]{1,0:T(4,128)S(1)} copy-done((s32[4,8]{1,0:T(4,128)S(1)}, s32[4,8]{1,0:T(4,128)}, u32[]{:S(2)}) %copy-start.2) | copy-done | bytes 152
  0.7 0.0 copy-start.1
  0.7 0.2 fusion
  0.9 0.5 copy-done.1
  1.3 0.0 copy-start
  1.3 0.9 %copy-done = bf16[512,256]{1,0:T(8,128)(2,1)S(1)} copy-done((bf16[512,256]{1,0:T(8,128)(2,1)S(1)}, bf16[512,256]{1,0:T(8,128)(2,1)}, u32[]{:S(2)}) %copy-start) | copy-done | bytes 262168
  2.3 51.7 %shard_map.37 = f32[4,32,128]{2,1,0:T(8,128)S(1)} custom-call(s32[16]{0:T(128)S(1)} %copy-done.1, bf16[512,256]{1,0:T(8,128)(2,1)S(1)} %copy-done), custom_call_target="tpu_custom_call" | custom-call | tf_op jit(solution)/shard_map/pallas_call | solution.py:306
  54.0 0.7 %broadcast_select_fusion = f32[4,32,128]{2,1,0:T(8,128)} fusion(f32[4,32,128]{2,1,0:T(8,128)S(1)} %shard_map.37, pred[4]{0:T(512)(128)(4,1)S(1)} %fusion), kind=kLoop, calls=%fused_computation | loop fusion | flops 16384 | bytes 131076 | tf_op jit(solution)/shard_map/jit(_where)/select_n | solution.py:337
Async XLA Ops:
  0.0 0.7 %copy-start.2 = (s32[4,8]{1,0:T(4,128)S(1)}, s32[4,8]{1,0:T(4,128)}, u32[]{:S(2)}) copy-start(s32[4,8]{1,0:T(4,128)} %param.5) | copy-start | bytes 388
  0.7 0.7 %copy-start.1 = (s32[16]{0:T(128)S(1)}, s32[16]{0:T(128)}, u32[]{:S(2)}) copy-start(s32[16]{0:T(128)} %plan_ref.1) | copy-start | bytes 196
  1.3 0.9 %copy-start = (bf16[512,256]{1,0:T(8,128)(2,1)S(1)}, bf16[512,256]{1,0:T(8,128)(2,1)}, u32[]{:S(2)}) copy-start(bf16[512,256]{1,0:T(8,128)(2,1)} %expr_ref.1) | copy-start | bytes 786436
